TPU v7x, 256 devices: a whole 4x4x8 slice. The times are simulated.
256 devices in a mesh: section: 2 (over y_lo), req: 16 (over x, y_hi, core), tp: 8 (over z).
Axes of the slice: x: 4, y: 4 (y_hi: 2, y_lo: 2; y = y_hi * 2 + y_lo), z: 8, core: 2. Of those that a mesh axis runs over, the one named last changes fastest.
Arguments:
- draft_rows: bfloat16 [1024, 8192], P('tp', 'req'), may hold values from -4 to 4
- norm_gain: bfloat16 [2, 8192], P('section', 'req'), may hold values from 0.099609375 to 1.8984375
- w_query: bfloat16 [2, 8192, 8192], P('section', 'req', 'tp'), may hold values from -0.0625 to 0.0625
- w_keyval: bfloat16 [2, 2, 8192, 1024], P('section', None, 'req', 'tp'), may hold values from -0.0625 to 0.0625
- w_out: bfloat16 [2, 8192, 8192], P('section', 'tp', 'req'), may hold values from -0.0625 to 0.0625
- kv_cache: bfloat16 [2, 16, 2, 4096, 1024], P('section', 'req', None, None, 'tp'), may hold values from -360 to 360
- tree_counts: int32 [16], P('req'), may hold values from 16 to 64, as said below
- cache_lengths: int32 [16], P('req'), may hold values from 512 to 4096, as said below
- tree_parents: int32 [16, 64], P('req'), may hold values from 0 to 62, as said below
Outputs:
- layer_outputs: bfloat16 [2, 1024, 8192], P('section', 'tp', 'req')
Inputs may be any that keep to these rules, and one draw needn't show every extreme that they name: Live rows of request r are its slots 0 to tree_counts[r] - 1; some request has all 64 live. Positions 0 to cache_lengths[r] - 1 are in use; some request uses all 4096. `tree_parents`: the parent of slot t > 0 is a slot below t; slot 0 names itself.
All inputs are finite; a program needn't handle non-finite values.
Results may differ from a plain program's by a relative error of at most 0.03.
Values may be sent and summed in bfloat16 or wider, within the bound.
A program may use at most 64 MiB of HBM per device.

v0:
```python
import jax
import jax.numpy as jnp
from jax import lax
from jax.sharding import PartitionSpec as P

D = 8192
HEAD_DIM = 128
TREE = 64


EPSILON = 1e-05


def passed_along(shard, axis, by):
    devices = lax.axis_size(axis)
    pairs = [(i, i + by) for i in range(devices) if 0 <= i + by < devices]
    return lax.ppermute(shard, axis, pairs)


def ancestors(parents):
    indices = jnp.arange(TREE, dtype=jnp.int32)
    links = (parents[:, None] == indices[None, :]).astype(jnp.float32)
    reach = jnp.minimum(links + jnp.eye(TREE, dtype=jnp.float32), 1.0)
    for sweep in range(max(1, (TREE - 1).bit_length())):
        reach = jnp.minimum(jnp.dot(reach, reach, precision=lax.Precision.HIGHEST), 1.0)
    return reach


def attend(query, key_new, value_new, cache_keys, cache_values, length, reach):
    tree = query.shape[0]
    cache_len = cache_keys.shape[0]
    kv_count = cache_keys.shape[1] // HEAD_DIM
    group = query.shape[1] // cache_keys.shape[1]
    heads = query.reshape(tree, kv_count, group, HEAD_DIM)
    old_keys = cache_keys.reshape(cache_len, kv_count, HEAD_DIM)
    old_values = cache_values.reshape(cache_len, kv_count, HEAD_DIM)
    new_keys = key_new.reshape(tree, kv_count, HEAD_DIM)
    new_values = value_new.reshape(tree, kv_count, HEAD_DIM)
    factor = HEAD_DIM ** (-0.5)
    score_cache = (
        jnp.einsum("tkgd,ckd->kgtc", heads, old_keys, preferred_element_type=jnp.float32) * factor
    )
    score_tree = (
        jnp.einsum("tkgd,skd->kgts", heads, new_keys, preferred_element_type=jnp.float32) * factor
    )
    in_use = jnp.arange(cache_len, dtype=jnp.int32) < length
    score_cache = jnp.where(in_use, score_cache, -jnp.inf)
    score_tree = jnp.where(reach > 0.5, score_tree, -jnp.inf)
    top = jnp.maximum(jnp.max(score_cache, axis=-1), jnp.max(score_tree, axis=-1))
    weight_cache = jnp.exp(score_cache - top[..., None])
    weight_tree = jnp.exp(score_tree - top[..., None])
    total = jnp.sum(weight_cache, axis=-1) + jnp.sum(weight_tree, axis=-1)
    mixed = jnp.einsum(
        "kgtc,ckd->tkgd",
        weight_cache.astype(jnp.bfloat16),
        old_values,
        preferred_element_type=jnp.float32,
    )
    mixed = mixed + jnp.einsum(
        "kgts,skd->tkgd",
        weight_tree.astype(jnp.bfloat16),
        new_values,
        preferred_element_type=jnp.float32,
    )
    mixed = mixed / jnp.transpose(total, (2, 0, 1))[..., None]
    return mixed.reshape(tree, kv_count * group * HEAD_DIM)


def body(
    draft_rows,
    norm_gain,
    w_query,
    w_keyval,
    w_out,
    kv_cache,
    tree_counts,
    cache_lengths,
    tree_parents,
):
    gain = norm_gain[0].astype(jnp.float32)
    w_o = w_out[0]
    cache = kv_cache[0]
    width_query = w_query.shape[2]
    width_kv = w_keyval.shape[3]
    w_all = jnp.concatenate([w_query[0], w_keyval[0, 0], w_keyval[0, 1]], axis=1)
    rows_tp = draft_rows.shape[0]
    total_rows = rows_tp * lax.axis_size("tp")
    owned = total_rows // lax.axis_size("req")
    requests = tree_counts.shape[0]
    reach = jax.vmap(ancestors)(tree_parents)
    live = (jnp.arange(TREE, dtype=jnp.int32)[None, :] < tree_counts[:, None]).astype(jnp.float32)

    def layer_core(full):
        rows_wide = full.astype(jnp.float32)
        squares = jnp.sum(rows_wide * rows_wide, axis=1)
        scaled = (rows_wide * gain).astype(jnp.bfloat16)
        squares_all = lax.psum(squares, "req")
        squares_own = lax.dynamic_slice_in_dim(squares_all, lax.axis_index("req") * owned, owned, 0)
        summed = lax.psum_scatter(
            jnp.dot(scaled, w_all, preferred_element_type=jnp.float32),
            "req",
            scatter_dimension=0,
            tiled=True,
        )
        summed = summed * lax.rsqrt(squares_own / D + EPSILON)[:, None]
        query = summed[:, :width_query].astype(jnp.bfloat16).reshape(requests, TREE, width_query)
        keys_new = (
            summed[:, width_query : width_query + width_kv]
            .astype(jnp.bfloat16)
            .reshape(requests, TREE, width_kv)
        )
        values_new = (
            summed[:, width_query + width_kv :]
            .astype(jnp.bfloat16)
            .reshape(requests, TREE, width_kv)
        )
        mixed = lax.map(
            lambda items: attend(*items),
            (query, keys_new, values_new, cache[:, 0], cache[:, 1], cache_lengths, reach),
        )
        attended = (mixed * live[:, :, None]).reshape(owned, width_query).astype(jnp.bfloat16)
        return jnp.dot(
            lax.all_gather(attended, "req", axis=0, tiled=True),
            w_o,
            preferred_element_type=jnp.float32,
        )

    def layer_shard(shard):
        full = lax.all_gather(shard, "tp", axis=0, tiled=True)
        partial_rows = layer_core(full)
        summed = lax.psum_scatter(partial_rows, "tp", scatter_dimension=0, tiled=True)
        return (summed + shard.astype(jnp.float32)).astype(jnp.bfloat16)

    first = layer_shard(draft_rows)
    handed = passed_along(first, "section", 1)
    second = layer_shard(handed)
    on_draft = lax.axis_index("section") == 0
    result = jnp.where(on_draft, first, second)
    return result[None]


def solution(mesh):
    placed = (
        P("tp", "req"),
        P("section", "req"),
        P("section", "req", "tp"),
        P("section", None, "req", "tp"),
        P("section", "tp", "req"),
        P("section", "req", None, None, "tp"),
        P("req"),
        P("req"),
        P("req", None),
    )
    return jax.shard_map(
        body, mesh=mesh, in_specs=placed, out_specs=P("section", "tp", "req"), check_vma=False
    )
```

profile of v0, /device:TPU:8, one launch (start us, length us, event | category | flops | bytes accessed | tf_op | source)
XLA Modules:
  0.0 533.0 jit_solution(12207520792418425994)
XLA Ops:
  6.5 0.7 all-gather.5.cloned.1.call-update
  7.3 0.7 mul.134
  8.0 1.0 slice_bitcast_fusion.7
  9.0 41.8 %all-gather.5.cloned.1.call-done = bf16[1024,512]{1,0:T(8,128)(2,1)} async-done(((bf16[128,512]{1,0:T(8,128)(2,1)}), bf16[1024,512]{1,0:T(8,128)(2,1)}) %all-gather.5.cloned.1.call-update) | async-done | bytes 1048592 | tf_op jit(solution)/shard_map/all_gather | solution.py:129
  50.8 5.4 %fusion.35 = f32[1024,1280]{1,0:T(8,128)} fusion(bf16[1024,512]{1,0:T(8,128)(2,1)} %all-gather.5.cloned.1.call-done, f32[512]{0:T(512)S(1)} %bitcast.183, bf16[512,128]{1,0:T(8,128)(2,1)S(1)} %get-tuple-element.44, bf16[512,128]{1,0:T(8,128)(2,1)S(1)} %get-tuple-element.43, bf16[512,1024]{1,0:T(8,128)(2,1)} %bitcast.186), kind=kOutput, calls=%fused_computation.47 | convolution fusion | flops 1347682304 | bytes 7604224 | tf_op jit(solution)/shard_map/dot_general | solution.py:100
  56.3 0.6 copy-done.16
  56.9 0.1 fusion.58
  57.0 0.2 convolution_minimum_fusion.5
  57.2 0.2 convolution_minimum_fusion.4
  57.4 0.2 convolution_minimum_fusion.3
  57.5 0.2 convolution_minimum_fusion.2
  57.7 0.2 convolution_minimum_fusion.1
  57.9 0.2 fusion.32
  58.0 0.1 copy.52
  59.4 0.5 compare_convert_fusion.2
  60.0 1.5 fusion.15
  61.5 33.2 %psum.14 = f32[1024]{0:T(1024)S(1)} all-reduce(f32[1024]{0:T(1024)S(1)} %fusion.15), channel_id=1, replica_groups=mesh['section'=2,'req'=16,'tp'=8] {'req'}, use_global_device_ids=true, to_apply=%region_2.0 | all-reduce | flops 1024 | bytes 8192 | tf_op jit(solution)/shard_map/psum | solution.py:97
  94.7 0.1 add_rsqrt_fusion.1
  94.7 51.9 %reduce-scatter.5.cloned.1.call-done = f32[64,1280]{1,0:T(8,128)} async-done(((f32[1024,1280]{1,0:T(8,128)}), f32[64,1280]{1,0:T(8,128)}) %reduce-scatter.5.cloned.1.call-update) | async-done | bytes 327696 | tf_op jit(solution)/shard_map/reduce_scatter | solution.py:99
  146.6 1.1 multiply_convert_fusion.1
  147.7 0.7 copy-done.5
  148.4 4.5 fusion.61
  153.0 0.7 copy.54
  153.6 1.0 fusion.62
  154.6 0.7 max.20
  155.3 0.1 copy.55
  155.4 5.4 %fusion.2 = f32[8,64]{0,1:T(8,128)} fusion(f32[1,8,64,4096]{3,1,2,0:T(8,128)} %get-tuple-element.59, f32[8,64]{0,1:T(8,128)S(1)} %copy.55), kind=kLoop, calls=%fused_computation.6 | loop fusion | flops 4193792 | bytes 8392704 | tf_op jit(solution)/shard_map/while/body/eval_jaxpr/reduce_sum | solution.py:52
  160.8 0.4 copy-done.1
  161.2 2.0 fusion.22
  163.2 0.7 fusion.45
  163.8 0.8 copy.58
  164.6 0.1 copy.65
  164.7 0.8 add_bitcast_fusion.1
  165.5 1.1 fusion.30
  166.7 1.4 fusion.44
  168.1 52.5 %all-gather.7.cloned.1.call-done = bf16[1024,1024]{1,0:T(8,128)(2,1)} async-done(((bf16[64,1024]{1,0:T(8,128)(2,1)}), bf16[1024,1024]{1,0:T(8,128)(2,1)}) %all-gather.7.cloned.1.call-update) | async-done | bytes 2097168 | tf_op jit(solution)/shard_map/all_gather | solution.py:123
  220.6 4.2 fusion.39
  224.8 41.9 %reduce-scatter.7.cloned.1.call-done = f32[128,512]{1,0:T(8,128)} async-done(((f32[1024,512]{1,0:T(8,128)}), f32[128,512]{1,0:T(8,128)}) %reduce-scatter.7.cloned.1.call-update) | async-done | bytes 262160 | tf_op jit(solution)/shard_map/reduce_scatter | solution.py:131
  266.7 1.0 add_convert_fusion.1
  267.7 1.3 collective-permute-start
  269.0 5.6 %collective-permute-done = bf16[128,512]{1,0:T(8,128)(2,1)S(1)} collective-permute-done((bf16[128,512]{1,0:T(8,128)(2,1)S(1)}, bf16[128,512]{1,0:T(8,128)(2,1)S(1)}, u32[]{:S(2)}, u32[]{:S(2)}) %collective-permute-start) | collective-permute-done | bytes 131104 | tf_op jit(solution)/shard_map/ppermute | solution.py:17
  274.6 0.6 copy-done.7
  275.3 37.6 %all-gather.9.cloned.1.call-done = bf16[1024,512]{1,0:T(8,128)(2,1)} async-done(((bf16[128,512]{1,0:T(8,128)(2,1)}), bf16[1024,512]{1,0:T(8,128)(2,1)}) %all-gather.9.cloned.1.call-update) | async-done | bytes 1048592 | tf_op jit(solution)/shard_map/all_gather | solution.py:129
  312.9 5.5 %fusion.33 = f32[1024,1280]{1,0:T(8,128)} fusion(bf16[1024,512]{1,0:T(8,128)(2,1)} %all-gather.9.cloned.1.call-done, f32[512]{0:T(512)S(1)} %bitcast.184, bf16[512,128]{1,0:T(8,128)(2,1)} %copy-done.12, bf16[512,128]{1,0:T(8,128)(2,1)} %copy-done.11, bf16[512,1024]{1,0:T(8,128)(2,1)} %bitcast.187), kind=kOutput, calls=%fused_computation.46 | convolution fusion | flops 1347682304 | bytes 7604224 | tf_op jit(solution)/shard_map/dot_general | solution.py:100
  318.5 1.5 fusion.17
  320.0 33.3 %psum.15 = f32[1024]{0:T(1024)S(1)} all-reduce(f32[1024]{0:T(1024)S(1)} %fusion.17), channel_id=1, replica_groups=mesh['section'=2,'req'=16,'tp'=8] {'req'}, use_global_device_ids=true, to_apply=%region_10.11 | all-reduce | flops 1024 | bytes 8192 | tf_op jit(solution)/shard_map/psum | solution.py:97
  353.3 0.1 add_rsqrt_fusion
  353.4 55.3 %reduce-scatter.9.cloned.1.call-done = f32[64,1280]{1,0:T(8,128)} async-done(((f32[1024,1280]{1,0:T(8,128)}), f32[64,1280]{1,0:T(8,128)}) %reduce-scatter.9.cloned.1.call-update) | async-done | bytes 327696 | tf_op jit(solution)/shard_map/reduce_scatter | solution.py:99
  408.7 1.1 multiply_convert_fusion
  409.9 0.6 copy-done.4
  410.5 0.3 fusion.64
  410.8 4.6 fusion.63
  415.4 0.1 copy.61
  415.5 4.8 fusion.4
  420.3 1.0 copy-done.2
  421.3 2.0 fusion.25
  423.3 0.1 copy.64
  423.4 0.1 copy.67
  423.6 1.1 fusion.31
  424.7 0.7 fusion.43
  425.6 52.5 %all-gather.11.cloned.1.call-done = bf16[1024,1024]{1,0:T(8,128)(2,1)} async-done(((bf16[64,1024]{1,0:T(8,128)(2,1)}), bf16[1024,1024]{1,0:T(8,128)(2,1)}) %all-gather.11.cloned.1.call-update) | async-done | bytes 2097168 | tf_op jit(solution)/shard_map/all_gather | solution.py:123
  478.1 4.1 fusion.37
  482.2 42.3 %reduce-scatter.11.cloned.1.call-done = f32[128,512]{1,0:T(8,128)} async-done(((f32[1024,512]{1,0:T(8,128)}), f32[128,512]{1,0:T(8,128)}) %reduce-scatter.11.cloned.1.call-update) | async-done | bytes 262160 | tf_op jit(solution)/shard_map/reduce_scatter | solution.py:131
  524.5 1.6 fusion.52
  (52 shorter events, 0.7 us)
Async XLA Ops:
  6.5 214.0 %copy-start = (bf16[1,1024,512]{2,1,0:T(8,128)(2,1)S(1)}, bf16[1,1024,512]{2,1,0:T(8,128)(2,1)}, u32[]{:S(2)}) copy-start(bf16[1,1024,512]{2,1,0:T(8,128)(2,1)} %param.13) | copy-start | bytes 3145732
  6.5 44.2 %all-gather.5.cloned.1.call-start = ((), (), s32[]{:S(2)}) async-start(), calls=%async_computation.4 | async-start | bytes 1179648 | tf_op jit(solution)/shard_map/all_gather | solution.py:129
  7.3 139.4 %reduce-scatter.5.cloned.1.call-start = ((), (), s32[]{:S(2)}) async-start(), calls=%async_computation.5 | async-start | bytes 5570560 | tf_op jit(solution)/shard_map/reduce_scatter | solution.py:99
  8.0 48.2 %copy-start.14 = (f32[1,512]{1,0:T(1,128)}, f32[1,512]{1,0:T(1,128)S(1)}, u32[]{:S(2)}) copy-start(f32[1,512]{1,0:T(1,128)S(1)} %mul.134) | copy-start | bytes 6148
  9.0 47.2 %copy-start.11 = (bf16[512,128]{1,0:T(8,128)(2,1)}, bf16[512,128]{1,0:T(8,128)(2,1)S(1)}, u32[]{:S(2)}) copy-start(bf16[512,128]{1,0:T(8,128)(2,1)S(1)} %get-tuple-element.43) | copy-start | bytes 393220
  9.0 47.2 %copy-start.12 = (bf16[512,128]{1,0:T(8,128)(2,1)}, bf16[512,128]{1,0:T(8,128)(2,1)S(1)}, u32[]{:S(2)}) copy-start(bf16[512,128]{1,0:T(8,128)(2,1)S(1)} %get-tuple-element.44) | copy-start | bytes 393220
  56.2 0.7 copy-start.16
  56.3 92.2 %copy-start.3 = (bf16[1,1,2,4096,128]{4,3,2,1,0:T(8,128)(2,1)S(1)}, bf16[1,1,2,4096,128]{4,3,2,1,0:T(8,128)(2,1)}, u32[]{:S(2)}) copy-start(bf16[1,1,2,4096,128]{4,3,2,1,0:T(8,128)(2,1)} %param.14) | copy-start | bytes 6291460
  56.3 164.3 %all-gather.7.cloned.1.call-start = ((), (), s32[]{:S(2)}) async-start(), calls=%async_computation.6 | async-start | bytes 2228224 | tf_op jit(solution)/shard_map/all_gather | solution.py:123
  147.7 0.7 copy-start.5
  155.4 5.8 %copy-start.1 = (f32[1,8,64,4096]{3,1,2,0:T(8,128)S(1)}, f32[1,8,64,4096]{3,1,2,0:T(8,128)}, u32[]{:S(2)}) copy-start(f32[1,8,64,4096]{3,1,2,0:T(8,128)} %get-tuple-element.59) | copy-start | bytes 25165828
  168.1 98.6 %copy-start.6 = (bf16[128,512]{1,0:T(8,128)(2,1)S(1)}, bf16[128,512]{1,0:T(8,128)(2,1)}, u32[]{:S(2)}) copy-start(bf16[128,512]{1,0:T(8,128)(2,1)} %param.9) | copy-start | bytes 393220
  168.1 98.6 %reduce-scatter.7.cloned.1.call-start = ((), (), s32[]{:S(2)}) async-start(), calls=%async_computation.7 | async-start | bytes 2359296 | tf_op jit(solution)/shard_map/reduce_scatter | solution.py:131
  224.8 88.1 %copy-start.15 = (f32[1,512]{1,0:T(1,128)S(1)}, f32[1,512]{1,0:T(1,128)}, u32[]{:S(2)}) copy-start(f32[1,512]{1,0:T(1,128)} %copy-done.14) | copy-start | bytes 6148
  224.8 88.1 %all-gather.9.cloned.1.call-start = ((), (), s32[]{:S(2)}) async-start(), calls=%async_computation.8 | async-start | bytes 1179648 | tf_op jit(solution)/shard_map/all_gather | solution.py:129
  267.7 142.2 %copy-start.9 = (bf16[128,512]{1,0:T(8,128)(2,1)}, bf16[128,512]{1,0:T(8,128)(2,1)S(1)}, u32[]{:S(2)}) copy-start(bf16[128,512]{1,0:T(8,128)(2,1)S(1)} %add_convert_fusion.1) | copy-start | bytes 393220
  267.7 6.9 %collective-permute-start = (bf16[128,512]{1,0:T(8,128)(2,1)S(1)}, bf16[128,512]{1,0:T(8,128)(2,1)S(1)}, u32[]{:S(2)}, u32[]{:S(2)}) collective-permute-start(bf16[128,512]{1,0:T(8,128)(2,1)S(1)} %add_convert_fusion.1), channel_id=1, source_target_pairs={{0,128},{1,129},{2,130},{3,131},{4,132},{5,133},{6,134},{7,135},{8... | collective-permute-start | bytes 393224 | tf_op jit(solution)/shard_map/ppermute | solution.py:17
  274.6 0.6 copy-start.7
  275.2 133.5 %reduce-scatter.9.cloned.1.call-start = ((), (), s32[]{:S(2)}) async-start(), calls=%async_computation.9 | async-start | bytes 5570560 | tf_op jit(solution)/shard_map/reduce_scatter | solution.py:99
  318.4 159.6 %all-gather.11.cloned.1.call-start = ((), (), s32[]{:S(2)}) async-start(), calls=%async_computation.10 | async-start | bytes 2228224 | tf_op jit(solution)/shard_map/all_gather | solution.py:123
  409.8 0.7 copy-start.4
  415.5 5.8 %copy-start.2 = (f32[1,8,64,4096]{3,1,2,0:T(8,128)S(1)}, f32[1,8,64,4096]{3,1,2,0:T(8,128)}, u32[]{:S(2)}) copy-start(f32[1,8,64,4096]{3,1,2,0:T(8,128)} %get-tuple-element.72) | copy-start | bytes 25165828
  421.3 3.5 copy-start.13
  425.5 99.0 %copy-start.8 = (bf16[128,512]{1,0:T(8,128)(2,1)S(1)}, bf16[128,512]{1,0:T(8,128)(2,1)}, u32[]{:S(2)}) copy-start(bf16[128,512]{1,0:T(8,128)(2,1)} %copy-done.7) | copy-start | bytes 393220
  425.5 99.0 %copy-start.10 = (bf16[128,512]{1,0:T(8,128)(2,1)S(1)}, bf16[128,512]{1,0:T(8,128)(2,1)}, u32[]{:S(2)}) copy-start(bf16[128,512]{1,0:T(8,128)(2,1)} %copy-done.9) | copy-start | bytes 393220
  425.5 99.0 %reduce-scatter.11.cloned.1.call-start = ((), (), s32[]{:S(2)}) async-start(), calls=%async_computation.11 | async-start | bytes 2359296 | tf_op jit(solution)/shard_map/reduce_scatter | solution.py:131
Sparse Core Ops, SparseCore 0:
  9.1 41.5 all-gather.4
  56.4 90.2 reduce-scatter.4
  168.2 52.3 all-gather.6
  224.9 41.7 reduce-scatter.6
  275.3 37.4 all-gather.8
  318.6 90.1 reduce-scatter.8
  425.6 52.4 all-gather.10
  482.4 42.1 reduce-scatter.10
where the time goes:
time: 534 us; the launch traced here: 533 us
  waiting for transfers between devices  382 us (72%)
  blocking collectives  66.5 us (12%)
  matrix products  36.9 us (7%)
  other arithmetic  23.7 us (4%)
  between operations  15.1 us (3%)
  local copies, waits for them, and re-layouts  7.07 us (1%)
    reduce_scatter x2, waiting for transfers between devices, layer_core(): lax.psum_scatter(jnp.dot(scaled, w_all, preferred_element_type=jnp.float3...  107 us
    all_gather x2, waiting for transfers between devices, layer_core(): lax.all_gather(attended, 'req', axis=0, tiled=True)  105 us
    reduce_scatter x2, waiting for transfers between devices, layer_shard(): lax.psum_scatter(partial_rows, 'tp', scatter_dimension=0, tiled=True)  84.2 us
    all_gather x2, waiting for transfers between devices, layer_shard(): full = lax.all_gather(shard, 'tp', axis=0, tiled=True)  79.4 us
    psum x2, blocking collectives, layer_core(): squares_all = lax.psum(squares, 'req')  66.5 us
    dot_general x2, matrix products, layer_core(): jnp.dot(scaled, w_all, preferred_element_type=jnp.float32)  10.9 us
    reduce_sum x4, other arithmetic, attend(): total = jnp.sum(weight_cache, axis=-1) + jnp.sum(weight_tree, axis=-1)  10.9 us
  transfers between devices with their start and end apart: 9, of which 9 were waited for; matrix products, arithmetic and copies ran while one was open for 1% of the time, Pallas kernels for 0%

commit v1 on v0

v1 whole, which is shorter than its diff:
```python
import functools

import jax
import jax.numpy as jnp
from jax import lax
from jax.experimental import pallas as pl
from jax.experimental.pallas import tpu as pltpu
from jax.sharding import PartitionSpec as P

MESH = pl.DeviceIdType.MESH
F32, BF16 = jnp.float32, jnp.bfloat16

D = 8192
HEAD_DIM = 128
TREE = 64
EPSILON = 1e-05

BATCHES = 4
SLOTS = TREE // BATCHES
OFFSET = 1
KEY_BLOCK = 1024
NX, NY, NZ = 4, 2, 8
CHIPS = NX * NY
OWN = 2
SCORE_SCALE = HEAD_DIM ** -0.5 * 1.4426950408889634
LOW = -1e30

ROWS1, ROWS2, ROWS_SIB, SUMS, SQUARES, HEADS, HEADS_SIB, OUT1, OUT2, HAND = range(10)


def dot(a, b):
    return jnp.dot(a, b, preferred_element_type=F32)


def dot_nt(a, b):
    return lax.dot_general(a, b, (((1,), (1,)), ((), ())), preferred_element_type=F32)


def kernel(
    draft, gain, w_query, w_keyval, w_out, cache, parents, counts, lengths, out,
    rows, gains, w_in, w_o, keys, values, values_t, part, sums, sq_send, sq_recv,
    keys_new, values_new, reach, scores, heads, outp, out1, merged, out2, handed,
    send, recv, local, sib_send, sib_recv,
):
    T = SLOTS
    sec = lax.axis_index("section")
    req = lax.axis_index("req")
    z = lax.axis_index("tp")
    chip, core = req // 2, req % 2
    x, y = chip // NY, chip % NY
    key_blocks, key_block = scores.shape[0], scores.shape[1]
    lanes = scores.shape[2]

    def along(by):
        return (sec, req, (z + by + NZ) % NZ)

    sibling = (sec, chip * 2 + (1 - core), z)

    def planar(dx, dy, dc):
        to_chip = ((x + dx) % NX) * NY + (y + dy) % NY
        to_core = (core + dc) % 2
        return to_chip, to_core, (sec, to_chip * 2 + to_core, z)

    other_section = (1 - sec, req, z)
    offsets = [(dx, dy) for dx in range(NX) for dy in range(NY)]
    near = (1, -1, 2, -2)

    def push(src, dst, phase, m, device):
        pltpu.make_async_remote_copy(
            src_ref=src, dst_ref=dst, send_sem=send.at[m, phase], recv_sem=recv.at[m, phase],
            device_id=device, device_id_type=MESH,
        ).start()

    def await_bytes(ref, sem):
        pltpu.make_async_copy(ref, ref, sem).wait()

    @pl.when(sec == 0)
    def _():
        for m in range(BATCHES):
            pltpu.make_async_copy(
                draft.at[:, pl.ds(m * T, T)], rows.at[m, core, OWN], recv.at[m, HAND]
            ).start()

    half = w_in.shape[2] - HEAD_DIM
    loads = [
        pltpu.make_async_copy(
            w_query.at[0, :, pl.ds(pl.multiple_of(core * half, 128), half)],
            w_in.at[core, :, pl.ds(0, half)], local.at[0]),
        pltpu.make_async_copy(
            w_keyval.at[0, core], w_in.at[core, :, pl.ds(half, HEAD_DIM)], local.at[1]),
        pltpu.make_async_copy(cache.at[0, 0, 1], values, local.at[2]),
        pltpu.make_async_copy(cache.at[0, 0, 0], keys, local.at[3]),
        pltpu.make_async_copy(w_out.at[0], w_o, local.at[4]),
    ]
    for load in loads:
        load.start()
    gains[core] = jnp.broadcast_to(gain[...].astype(F32), gains.shape[1:])

    barrier = pltpu.get_barrier_semaphore()
    partners = [along(by) for by in near] + [sibling, other_section]
    partners += [planar(dx, dy, dc)[2] for dx, dy in offsets if (dx, dy) != (0, 0) for dc in range(2)]
    for device in partners:
        pl.semaphore_signal(barrier, inc=1, device_id=device, device_id_type=MESH)
    pl.semaphore_wait(barrier, len(partners))

    def step_rows(m):
        await_bytes(rows.at[0, 0, 0], recv.at[m, HAND])
        for by in near:
            push(rows.at[m, core, OWN], rows.at[m, core, OWN - by], ROWS1, m, along(by))

    @pl.when(sec == 0)
    def _():
        def each(m, carry):
            step_rows(m)
            return carry
        lax.fori_loop(0, BATCHES, each, 0)

    to_sibling = [
        pltpu.make_async_remote_copy(
            src_ref=gains.at[core], dst_ref=gains.at[core], send_sem=sib_send.at[0], recv_sem=sib_recv.at[0],
            device_id=sibling, device_id_type=MESH),
        pltpu.make_async_remote_copy(
            src_ref=w_query.at[0, :, pl.ds(pl.multiple_of((1 - core) * half, 128), half)],
            dst_ref=w_in.at[core, :, pl.ds(0, half)], send_sem=sib_send.at[1], recv_sem=sib_recv.at[1],
            device_id=sibling, device_id_type=MESH),
        pltpu.make_async_remote_copy(
            src_ref=w_keyval.at[0, 1 - core], dst_ref=w_in.at[core, :, pl.ds(half, HEAD_DIM)],
            send_sem=sib_send.at[2], recv_sem=sib_recv.at[2], device_id=sibling, device_id_type=MESH),
    ]
    for copy in to_sibling:
        copy.start()

    row_index = lax.broadcasted_iota(jnp.int32, (TREE, TREE), 0)
    col_index = lax.broadcasted_iota(jnp.int32, (TREE, TREE), 1)
    closure = jnp.where((parents[...] == row_index) | (row_index == col_index), 1.0, 0.0)
    for _ in range(6):
        closure = jnp.minimum(dot(closure.astype(BF16), closure.astype(BF16)), 1.0)
    reach[...] = closure.astype(BF16)
    keys_new[...] = jnp.zeros_like(keys_new)
    values_new[...] = jnp.zeros_like(values_new)

    diagonal = lax.broadcasted_iota(jnp.int32, (HEAD_DIM, HEAD_DIM), 0) == lax.broadcasted_iota(
        jnp.int32, (HEAD_DIM, HEAD_DIM), 1)
    identity = jnp.where(diagonal, 1.0, 0.0).astype(BF16)
    loads[2].wait()

    def turn(b, carry):
        values_t[b] = dot_nt(identity, values[pl.ds(pl.multiple_of(b * key_block, key_block), key_block), :]).astype(BF16)
        return carry
    lax.fori_loop(0, key_blocks, turn, 0)
    loads[3].wait()
    loads[4].wait()
    loads[0].wait()
    loads[1].wait()
    for copy in to_sibling:
        copy.wait()

    length = lengths[0]
    count = counts[0]

    def step_pass(m):
        await_bytes(rows.at[0, 0, pl.ds(0, 4)], recv.at[m, ROWS1])
        push(rows.at[m, core, 0], rows.at[m, core, 7], ROWS2, m, along(1))
        push(rows.at[m, core, 4], rows.at[m, core, 5], ROWS2, m, along(-1))
        push(rows.at[m, core, 0, 0], rows.at[m, core, 6, 0], ROWS2, m, along(2))
        push(rows.at[m, core, 4, 1], rows.at[m, core, 6, 1], ROWS2, m, along(-2))
        push(rows.at[m, core, pl.ds(0, 5)], rows.at[m, core, pl.ds(0, 5)], ROWS_SIB, m, sibling)

    def step_last_rows(m):
        await_bytes(rows.at[0, 0, pl.ds(0, 3)], recv.at[m, ROWS2])
        push(rows.at[m, core, pl.ds(5, 3)], rows.at[m, core, pl.ds(5, 3)], ROWS_SIB, m, sibling)

    def step_project(m):
        await_bytes(rows.at[0, 0], recv.at[m, ROWS_SIB])
        total_sq = None
        total = None
        for s in range(2):
            block = rows[m, s].reshape(CHIPS * 2 * T, rows.shape[-1]).astype(F32)
            sq = jnp.sum(block * block, axis=1, keepdims=True)
            scaled = (block * gains[s, 0:1, :]).astype(BF16)
            product = dot(scaled, w_in[s])
            total = product if total is None else total + product
            total_sq = sq if total_sq is None else total_sq + sq
        part[m] = total.reshape(CHIPS, 2, T, total.shape[1]).astype(BF16)
        wide = jnp.broadcast_to(total_sq, (CHIPS * 2 * T, HEAD_DIM))
        lane = lax.broadcasted_iota(jnp.int32, wide.shape, 1)
        high = wide.astype(BF16)
        low = (wide - high.astype(F32)).astype(BF16)
        packed = jnp.where(lane == 0, high.astype(F32), jnp.where(lane == 1, low.astype(F32), 0.0))
        sq_send[m] = packed.reshape(CHIPS, 2, T, HEAD_DIM).astype(BF16)
        for dx, dy in offsets:
            for dc in range(2):
                if (dx, dy, dc) == (0, 0, 0):
                    continue
                to_chip, to_core, device = planar(dx, dy, dc)
                place = (to_chip - z + OWN + NZ) % NZ
                push(part.at[m, place, to_core], sums.at[m, dc * CHIPS + dx * NY + dy], SUMS, m, device)
                if dc == 0:
                    push(sq_send.at[m, place, to_core], sq_recv.at[m, dx * NY + dy], SQUARES, m, device)

    def step_attend(m):
        await_bytes(sums.at[0, pl.ds(0, 15)], recv.at[m, SUMS])
        await_bytes(sq_recv.at[0, pl.ds(0, 7)], recv.at[m, SQUARES])
        place = (chip - z + OWN + NZ) % NZ
        same = part[m, place, core].astype(F32)
        squares = sq_send[m, place, core].astype(F32)
        for k in range(1, CHIPS):
            same = same + sums[m, k].astype(F32)
            squares = squares + sq_recv[m, k].astype(F32)
        other = sums[m, CHIPS].astype(F32)
        for k in range(CHIPS + 1, 2 * CHIPS):
            other = other + sums[m, k].astype(F32)
        inverse = lax.rsqrt(jnp.sum(squares, axis=1, keepdims=True) / D + EPSILON)
        same = same * inverse
        other = other * inverse
        first = jnp.where(core == 0, same, other).astype(BF16)
        second = jnp.where(core == 0, other, same).astype(BF16)
        query = jnp.concatenate(
            [g[:, h * HEAD_DIM:(h + 1) * HEAD_DIM] for g in (first, second) for h in range(half // HEAD_DIM)], axis=0)
        slots = pl.ds(pl.multiple_of(m * T, T), T)
        keys_new[slots, :] = first[:, half:]
        values_new[slots, :] = second[:, half:]

        lane_slot = lax.broadcasted_iota(jnp.int32, (TREE, lanes), 1) % T + m * T
        pick = jnp.where(lax.broadcasted_iota(jnp.int32, (TREE, lanes), 0) == lane_slot, 1.0, 0.0).astype(BF16)
        reached = dot(reach[...], pick) > 0.5
        tree_scores = jnp.where(reached, dot_nt(keys_new[...], query), LOW)
        top = jnp.max(tree_scores, axis=0, keepdims=True)
        position = lax.broadcasted_iota(jnp.int32, (key_block, lanes), 0)
        for b in range(key_blocks):
            block = dot_nt(keys[b * key_block:(b + 1) * key_block, :], query)
            block = jnp.where(position < length - b * key_block, block, LOW)
            scores[b] = block
            top = jnp.maximum(top, jnp.max(block, axis=0, keepdims=True))
        weights = jnp.exp2((tree_scores - top) * SCORE_SCALE)
        total = jnp.sum(weights, axis=0, keepdims=True)
        values_new_t = dot_nt(identity, values_new[...]).astype(BF16)
        mixed = dot(values_new_t, weights.astype(BF16))
        for b in range(key_blocks):
            weights = jnp.exp2((scores[b] - top) * SCORE_SCALE)
            total = total + jnp.sum(weights, axis=0, keepdims=True)
            mixed = mixed + dot(values_t[b], weights.astype(BF16))
        live = lax.broadcasted_iota(jnp.int32, (1, lanes), 1) % T + m * T < count
        mixed = jnp.where(live, mixed / total, 0.0).T.astype(BF16)
        for h in range(lanes // T):
            heads[m, core, chip, :, h * HEAD_DIM:(h + 1) * HEAD_DIM] = mixed[h * T:(h + 1) * T, :]
        for dx, dy in offsets:
            if (dx, dy) != (0, 0):
                push(heads.at[m, core, chip], heads.at[m, core, chip], HEADS, m, planar(dx, dy, 0)[2])

    def step_heads(m):
        await_bytes(heads.at[0, 0, pl.ds(0, 7)], recv.at[m, HEADS])
        push(heads.at[m, core], heads.at[m, core], HEADS_SIB, m, sibling)

    def step_out(m):
        await_bytes(heads.at[0, 0], recv.at[m, HEADS_SIB])
        product = dot(heads[m].reshape(2 * CHIPS * T, heads.shape[-1]), w_o[...]).astype(BF16)
        product = product.reshape(2, CHIPS, T, product.shape[1])
        for i in range(2):
            outp[m, :, i] = product[i]
        push(outp.at[m, (z + 3) % NZ], out1.at[m, 0], OUT1, m, along(1))
        push(outp.at[m, (z + 5) % NZ], out1.at[m, 1], OUT1, m, along(-1))
        push(outp.at[m, (z + 4) % NZ, 0], out1.at[m, 2, 0], OUT1, m, along(2))
        push(outp.at[m, (z + 4) % NZ, 1], out1.at[m, 2, 1], OUT1, m, along(-2))
        push(outp.at[m, (z + 1) % NZ], out2.at[m, 2], OUT2, m, along(1))
        push(outp.at[m, (z + 7) % NZ], out2.at[m, 3], OUT2, m, along(-1))

    def step_merge(m):
        await_bytes(out1.at[0], recv.at[m, OUT1])
        for side, by in enumerate((2, -2)):
            both = outp[m, (z + by + NZ) % NZ].astype(F32) + out1[m, side].astype(F32)
            merged[m, side] = both.astype(BF16)
            merged[m, side, side] = (both[side] + out1[m, 2, side].astype(F32)).astype(BF16)
            push(merged.at[m, side], out2.at[m, side], OUT2, m, along(by))

    def step_finish(m):
        await_bytes(out2.at[0], recv.at[m, OUT2])
        total = outp[m, z].astype(F32)
        for k in range(4):
            total = total + out2[m, k].astype(F32)
        result = (total + rows[m, core, OWN].astype(F32)).astype(BF16)
        out[:, pl.ds(pl.multiple_of(m * T, T), T), :] = result

        @pl.when(sec == 0)
        def _():
            handed[m] = result
            push(handed.at[m], rows.at[m, core, OWN], HAND, m, other_section)

    def step_rows_handed(m):
        @pl.when(sec == 1)
        def _():
            step_rows(m)

    steps = [step_rows_handed, step_pass, step_last_rows, step_project, step_attend,
             step_heads, step_out, step_merge, step_finish]

    def tick(t, carry):
        for k in reversed(range(len(steps))):
            since = t - k
            run = (since >= 0) & (since <= (BATCHES - 1) * OFFSET)
            if OFFSET > 1:
                run = run & (since % OFFSET == 0)

            @pl.when(run)
            def _(k=k, since=since):
                steps[k](since // OFFSET)
        return carry
    lax.fori_loop(0, len(steps) + (BATCHES - 1) * OFFSET, tick, 0)

    def drain(m, carry):
        await_bytes(rows.at[0, 0, pl.ds(0, 4)], send.at[m, ROWS1])
        await_bytes(rows.at[0, 0, pl.ds(0, 3)], send.at[m, ROWS2])
        await_bytes(rows.at[0, 0], send.at[m, ROWS_SIB])
        await_bytes(sums.at[0, pl.ds(0, 15)], send.at[m, SUMS])
        await_bytes(sq_recv.at[0, pl.ds(0, 7)], send.at[m, SQUARES])
        await_bytes(heads.at[0, 0, pl.ds(0, 7)], send.at[m, HEADS])
        await_bytes(heads.at[0, 0], send.at[m, HEADS_SIB])
        await_bytes(out1.at[0], send.at[m, OUT1])
        await_bytes(out2.at[0], send.at[m, OUT2])

        @pl.when(sec == 0)
        def _():
            await_bytes(handed.at[0], send.at[m, HAND])
        return carry
    lax.fori_loop(0, BATCHES, drain, 0)


def body(draft_rows, norm_gain, w_query, w_keyval, w_out, kv_cache, tree_counts, cache_lengths, tree_parents):
    T, N = SLOTS, BATCHES
    feats = draft_rows.shape[1]
    width = w_query.shape[2]
    positions = kv_cache.shape[3]
    half = width // 2 + HEAD_DIM
    lanes = width // HEAD_DIM * T
    blocks = positions // KEY_BLOCK
    vmem = pl.BlockSpec(memory_space=pltpu.VMEM)
    smem = pl.BlockSpec(memory_space=pltpu.SMEM)
    anywhere = pl.BlockSpec(memory_space=pl.ANY)
    result = pl.pallas_call(
        kernel,
        out_shape=jax.ShapeDtypeStruct((2, TREE, feats), BF16),
        in_specs=[anywhere, vmem, anywhere, anywhere, anywhere, anywhere, vmem, smem, smem],
        out_specs=vmem,
        scratch_shapes=[
            pltpu.VMEM((N, 2, NZ, 2, T, feats), BF16),
            pltpu.VMEM((2, 8, feats), F32),
            pltpu.VMEM((2, feats, half), BF16),
            pltpu.VMEM((width, feats), BF16),
            pltpu.VMEM((positions, HEAD_DIM), BF16),
            pltpu.VMEM((positions, HEAD_DIM), BF16),
            pltpu.VMEM((blocks, HEAD_DIM, KEY_BLOCK), BF16),
            pltpu.VMEM((N, CHIPS, 2, T, half), BF16),
            pltpu.VMEM((N, 2 * CHIPS, T, half), BF16),
            pltpu.VMEM((N, CHIPS, 2, T, HEAD_DIM), BF16),
            pltpu.VMEM((N, CHIPS, T, HEAD_DIM), BF16),
            pltpu.VMEM((TREE, HEAD_DIM), BF16),
            pltpu.VMEM((TREE, HEAD_DIM), BF16),
            pltpu.VMEM((TREE, TREE), BF16),
            pltpu.VMEM((blocks, KEY_BLOCK, lanes), F32),
            pltpu.VMEM((N, 2, CHIPS, T, width), BF16),
            pltpu.VMEM((N, NZ, 2, T, feats), BF16),
            pltpu.VMEM((N, 3, 2, T, feats), BF16),
            pltpu.VMEM((N, 2, 2, T, feats), BF16),
            pltpu.VMEM((N, 4, 2, T, feats), BF16),
            pltpu.VMEM((N, 2, T, feats), BF16),
            pltpu.SemaphoreType.DMA((N, 10)),
            pltpu.SemaphoreType.DMA((N, 10)),
            pltpu.SemaphoreType.DMA((5,)),
            pltpu.SemaphoreType.DMA((3,)),
            pltpu.SemaphoreType.DMA((3,)),
        ],
        compiler_params=pltpu.CompilerParams(
            collective_id=0, has_side_effects=True, vmem_limit_bytes=40 << 20),
        name="two_layers",
    )(
        draft_rows.reshape(2, TREE, feats), norm_gain, w_query, w_keyval, w_out, kv_cache,
        tree_parents, tree_counts, cache_lengths,
    )
    return result.reshape(1, 2 * TREE, feats)


def solution(mesh):
    placed = (
        P("tp", "req"),
        P("section", "req"),
        P("section", "req", "tp"),
        P("section", None, "req", "tp"),
        P("section", "tp", "req"),
        P("section", "req", None, None, "tp"),
        P("req"),
        P("req"),
        P("req", None),
    )
    return jax.shard_map(
        body, mesh=mesh, in_specs=placed, out_specs=P("section", "tp", "req"), check_vma=False
    )
```

time: 534 us -> 155 us (0.29)
  waiting for transfers between devices: 382 us -> 0 us
  Pallas kernels: 0 us -> 146 us
  blocking collectives: 66.5 us -> 0 us
  matrix products: 36.9 us -> 0 us
  other arithmetic: 23.7 us -> 0 us
  between operations: 15.1 us -> 1.32 us
    reduce_scatter x4 -> x0, waiting for transfers between devices: 191 us -> none  [the longest x2 107 us: layer_core(): lax.psum_scatter(jnp.dot(scaled, w_all, preferred_element_type=jnp.float3...]
    all_gather x4 -> x0, waiting for transfers between devices: 184 us -> none  [the longest x2 105 us: layer_core(): lax.all_gather(attended, 'req', axis=0, tiled=True)]
    pallas_call x0 -> x1, Pallas kernels: none -> 146 us  [body(): pl.pallas_call(kernel, out_shape=jax.ShapeDtypeStruct((2, TREE, feats), B...]
    psum x2 -> x0, blocking collectives: 66.5 us -> none  [layer_core(): squares_all = lax.psum(squares, 'req')]
    dot_general x18 -> x0, matrix products: 36.9 us -> none  [the longest x2 10.9 us: layer_core(): jnp.dot(scaled, w_all, preferred_element_type=jnp.float32)]
    reduce_sum x6 -> x0, other arithmetic: 13.9 us -> none  [the longest x4 10.9 us: attend(): total = jnp.sum(weight_cache, axis=-1) + jnp.sum(weight_tree, axis=-1)]
    ppermute x1 -> x0, waiting for transfers between devices: 5.56 us -> none  [passed_along(): return lax.ppermute(shard, axis, pairs)]
  transfers between devices with their start and end apart: 9 -> 0, of which waited for: 9 -> 0; matrix products, arithmetic and copies ran while one was open for 1% -> 0% of each run, Pallas kernels for 0% -> 0%
where the time goes in v1:
time: 155 us
  Pallas kernels  146 us (94%)
  local copies, waits for them, and re-layouts  7.88 us (5%)
    pallas_call x1, Pallas kernels, body(): pl.pallas_call(kernel, out_shape=jax.ShapeDtypeStruct((2, TREE, feats), B...  146 us
    unnamed x15, local copies, waits for them, and re-layouts  7.88 us

profile of v1, /device:TPU:8, one launch (start us, length us, event | category | flops | bytes accessed | tf_op | source)
XLA Modules:
  0.0 154.8 jit_solution(8728662199560873376)
XLA Ops:
  1.3 0.0 copy-start
  1.3 1.6 %copy-done = bf16[1,1,2,4096,128]{4,3,2,1,0:T(8,128)(2,1)S(1)} copy-done((bf16[1,1,2,4096,128]{4,3,2,1,0:T(8,128)(2,1)S(1)}, bf16[1,1,2,4096,128]{4,3,2,1,0:T(8,128)(2,1)}, u32[]{:S(2)}) %copy-start) | copy-done | bytes 2097176
  2.9 0.0 copy-start.1
  2.9 1.2 copy-done.1
  4.1 0.0 copy-start.2
  4.1 1.2 copy-done.2
  5.3 0.0 copy-start.3
  5.3 0.9 copy-done.3
  6.3 0.0 copy-start.4
  6.3 0.9 copy-done.4
  7.2 0.0 copy-start.5
  7.2 0.7 copy-done.5
  7.9 0.0 copy-start.6
  7.9 0.7 copy-done.6
  8.5 145.6 %two_layers.1 = bf16[2,64,512]{2,1,0:T(8,128)(2,1)S(1)} custom-call(bf16[2,64,512]{2,1,0:T(8,128)(2,1)S(1)} %bitcast.3, bf16[1,512]{1,0:T(2,128)(2,1)S(1)} %copy-done.5, bf16[1,512,1024]{2,1,0:T(8,128)(2,1)S(1)} %copy-done.1, bf16[1,2,512,128]{3,2,1,0:T(8,128)(2,1)S(1)} %copy-done.3, bf16[1,1024,512]{2,1,0:T(8,128)(2,1)S(1)} %copy-done.2, ...), custom_call_target="tpu_custom_call" | custom-call | tf_op jit(solution)/shard_map/two_layers/pallas_call | solution.py:339
  154.2 0.7 copy.13
Async XLA Ops:
  1.3 1.6 %copy-start = (bf16[1,1,2,4096,128]{4,3,2,1,0:T(8,128)(2,1)S(1)}, bf16[1,1,2,4096,128]{4,3,2,1,0:T(8,128)(2,1)}, u32[]{:S(2)}) copy-start(bf16[1,1,2,4096,128]{4,3,2,1,0:T(8,128)(2,1)} %cache.1) | copy-start | bytes 6291460
  2.9 1.2 copy-start.1
  4.1 1.2 copy-start.2
  5.3 0.9 copy-start.3
  6.3 0.9 copy-start.4
  7.2 0.7 copy-start.5
  7.9 0.7 copy-start.6

commit v2 on v1

--- a/solution.py
+++ b/solution.py
@@ -17,7 +17,8 @@
 
 BATCHES = 4
 SLOTS = TREE // BATCHES
-OFFSET = 1
+PLACES = (0, 3, 6, 7, 14, 21, 23, 26, 30)
+OFFSET = 2
 KEY_BLOCK = 1024
 NX, NY, NZ = 4, 2, 8
 CHIPS = NX * NY
@@ -37,8 +38,8 @@
 
 
 def kernel(
-    draft, gain, w_query, w_keyval, w_out, cache, parents, counts, lengths, out,
-    rows, gains, w_in, w_o, keys, values, values_t, part, sums, sq_send, sq_recv,
+    draft, gain, w_query, w_keyval, w_out, cache, parents_in, counts, lengths, out,
+    parents, rows, gains, w_in, w_o, keys, values, values_t, part, sums, sq_send, sq_recv,
     keys_new, values_new, reach, scores, heads, outp, out1, merged, out2, handed,
     send, recv, local, sib_send, sib_recv,
 ):
@@ -91,6 +92,7 @@
         pltpu.make_async_copy(cache.at[0, 0, 1], values, local.at[2]),
         pltpu.make_async_copy(cache.at[0, 0, 0], keys, local.at[3]),
         pltpu.make_async_copy(w_out.at[0], w_o, local.at[4]),
+        pltpu.make_async_copy(parents_in, parents, local.at[5]),
     ]
     for load in loads:
         load.start()
@@ -107,13 +109,6 @@
         await_bytes(rows.at[0, 0, 0], recv.at[m, HAND])
         for by in near:
             push(rows.at[m, core, OWN], rows.at[m, core, OWN - by], ROWS1, m, along(by))
-
-    @pl.when(sec == 0)
-    def _():
-        def each(m, carry):
-            step_rows(m)
-            return carry
-        lax.fori_loop(0, BATCHES, each, 0)
 
     to_sibling = [
         pltpu.make_async_remote_copy(
@@ -130,30 +125,35 @@
     for copy in to_sibling:
         copy.start()
 
-    row_index = lax.broadcasted_iota(jnp.int32, (TREE, TREE), 0)
-    col_index = lax.broadcasted_iota(jnp.int32, (TREE, TREE), 1)
-    closure = jnp.where((parents[...] == row_index) | (row_index == col_index), 1.0, 0.0)
-    for _ in range(6):
-        closure = jnp.minimum(dot(closure.astype(BF16), closure.astype(BF16)), 1.0)
-    reach[...] = closure.astype(BF16)
-    keys_new[...] = jnp.zeros_like(keys_new)
-    values_new[...] = jnp.zeros_like(values_new)
-
     diagonal = lax.broadcasted_iota(jnp.int32, (HEAD_DIM, HEAD_DIM), 0) == lax.broadcasted_iota(
         jnp.int32, (HEAD_DIM, HEAD_DIM), 1)
     identity = jnp.where(diagonal, 1.0, 0.0).astype(BF16)
-    loads[2].wait()
-
-    def turn(b, carry):
-        values_t[b] = dot_nt(identity, values[pl.ds(pl.multiple_of(b * key_block, key_block), key_block), :]).astype(BF16)
-        return carry
-    lax.fori_loop(0, key_blocks, turn, 0)
-    loads[3].wait()
-    loads[4].wait()
-    loads[0].wait()
-    loads[1].wait()
-    for copy in to_sibling:
-        copy.wait()
+
+    def weights_ready():
+        loads[0].wait()
+        loads[1].wait()
+        for copy in to_sibling:
+            copy.wait()
+
+    def prepare():
+        loads[5].wait()
+        row_index = lax.broadcasted_iota(jnp.int32, (TREE, TREE), 0)
+        col_index = lax.broadcasted_iota(jnp.int32, (TREE, TREE), 1)
+        closure = jnp.where((parents[...] == row_index) | (row_index == col_index), 1.0, 0.0)
+        for _ in range(6):
+            closure = jnp.minimum(dot(closure.astype(BF16), closure.astype(BF16)), 1.0)
+        reach[...] = closure.astype(BF16)
+        keys_new[...] = jnp.zeros_like(keys_new)
+        values_new[...] = jnp.zeros_like(values_new)
+
+        loads[2].wait()
+
+        def turn(b, carry):
+            values_t[b] = dot_nt(identity, values[pl.ds(pl.multiple_of(b * key_block, key_block), key_block), :]).astype(BF16)
+            return carry
+        lax.fori_loop(0, key_blocks, turn, 0)
+        loads[3].wait()
+        loads[4].wait()
 
     length = lengths[0]
     count = counts[0]
@@ -172,6 +172,7 @@
 
     def step_project(m):
         await_bytes(rows.at[0, 0], recv.at[m, ROWS_SIB])
+        pl.when(m == 0)(weights_ready)
         total_sq = None
         total = None
         for s in range(2):
@@ -199,6 +200,7 @@
                     push(sq_send.at[m, place, to_core], sq_recv.at[m, dx * NY + dy], SQUARES, m, device)
 
     def step_attend(m):
+        pl.when(m == 0)(prepare)
         await_bytes(sums.at[0, pl.ds(0, 15)], recv.at[m, SUMS])
         await_bytes(sq_recv.at[0, pl.ds(0, 7)], recv.at[m, SQUARES])
         place = (chip - z + OWN + NZ) % NZ
@@ -286,17 +288,12 @@
             handed[m] = result
             push(handed.at[m], rows.at[m, core, OWN], HAND, m, other_section)
 
-    def step_rows_handed(m):
-        @pl.when(sec == 1)
-        def _():
-            step_rows(m)
-
-    steps = [step_rows_handed, step_pass, step_last_rows, step_project, step_attend,
+    steps = [step_rows, step_pass, step_last_rows, step_project, step_attend,
              step_heads, step_out, step_merge, step_finish]
 
     def tick(t, carry):
         for k in reversed(range(len(steps))):
-            since = t - k
+            since = t - PLACES[k]
             run = (since >= 0) & (since <= (BATCHES - 1) * OFFSET)
             if OFFSET > 1:
                 run = run & (since % OFFSET == 0)
@@ -305,7 +302,7 @@
             def _(k=k, since=since):
                 steps[k](since // OFFSET)
         return carry
-    lax.fori_loop(0, len(steps) + (BATCHES - 1) * OFFSET, tick, 0)
+    lax.fori_loop(0, PLACES[-1] + (BATCHES - 1) * OFFSET + 1, tick, 0)
 
     def drain(m, carry):
         await_bytes(rows.at[0, 0, pl.ds(0, 4)], send.at[m, ROWS1])
@@ -335,13 +332,14 @@
     blocks = positions // KEY_BLOCK
     vmem = pl.BlockSpec(memory_space=pltpu.VMEM)
     smem = pl.BlockSpec(memory_space=pltpu.SMEM)
-    anywhere = pl.BlockSpec(memory_space=pl.ANY)
+    anywhere = pl.BlockSpec(memory_space=pltpu.HBM)
     result = pl.pallas_call(
         kernel,
         out_shape=jax.ShapeDtypeStruct((2, TREE, feats), BF16),
-        in_specs=[anywhere, vmem, anywhere, anywhere, anywhere, anywhere, vmem, smem, smem],
+        in_specs=[anywhere, vmem, anywhere, anywhere, anywhere, anywhere, anywhere, smem, smem],
         out_specs=vmem,
         scratch_shapes=[
+            pltpu.VMEM((1, TREE), jnp.int32),
             pltpu.VMEM((N, 2, NZ, 2, T, feats), BF16),
             pltpu.VMEM((2, 8, feats), F32),
             pltpu.VMEM((2, feats, half), BF16),
@@ -365,12 +363,12 @@
             pltpu.VMEM((N, 2, T, feats), BF16),
             pltpu.SemaphoreType.DMA((N, 10)),
             pltpu.SemaphoreType.DMA((N, 10)),
-            pltpu.SemaphoreType.DMA((5,)),
+            pltpu.SemaphoreType.DMA((6,)),
             pltpu.SemaphoreType.DMA((3,)),
             pltpu.SemaphoreType.DMA((3,)),
         ],
         compiler_params=pltpu.CompilerParams(
-            collective_id=0, has_side_effects=True, vmem_limit_bytes=40 << 20),
+            collective_id=0, has_side_effects=True, vmem_limit_bytes=58 << 20),
         name="two_layers",
     )(
         draft_rows.reshape(2, TREE, feats), norm_gain, w_query, w_keyval, w_out, kv_cache,

time: 155 us -> 118 us (0.76)
  Pallas kernels: 146 us -> 115 us
  local copies, waits for them, and re-layouts: 7.88 us -> 1.57 us
    pallas_call x1, Pallas kernels: 146 us -> 115 us  [body(): pl.pallas_call(kernel, out_shape=jax.ShapeDtypeStruct((2, TREE, feats), B...]
    unnamed x15 -> x1, local copies, waits for them, and re-layouts: 7.88 us -> 1.57 us
where the time goes in v2:
time: 118 us
  Pallas kernels  115 us (97%)
  local copies, waits for them, and re-layouts  1.57 us (1%)
  between operations  1.3 us (1%)
    pallas_call x1, Pallas kernels, body(): pl.pallas_call(kernel, out_shape=jax.ShapeDtypeStruct((2, TREE, feats), B...  115 us

profile of v2, /device:TPU:8, one launch (start us, length us, event | category | flops | bytes accessed | tf_op | source)
XLA Modules:
  0.0 117.7 jit_solution(15401829142740485857)
XLA Ops:
  1.3 114.9 %two_layers.1 = bf16[2,64,512]{2,1,0:T(8,128)(2,1)} custom-call(bf16[2,64,512]{2,1,0:T(8,128)(2,1)} %bitcast.3, bf16[1,512]{1,0:T(2,128)(2,1)} %gain.1, bf16[1,512,1024]{2,1,0:T(8,128)(2,1)} %w_query.1, bf16[1,2,512,128]{3,2,1,0:T(8,128)(2,1)} %w_keyval.1, bf16[1,1024,512]{2,1,0:T(8,128)(2,1)} %w_out.1, bf16[1,1,2,4096,128]{4,3,2,1,0:T(8,128)(2,1)} %cache.1, ...), custom_call_target="tpu_custom_call" | custom-call | tf_op jit(solution)/shard_map/two_layers/pallas_call | solution.py:336
  116.2 1.6 %copy.13 = bf16[1,128,512]{2,1,0:T(8,128)(2,1)} copy(bf16[1,128,512]{2,1,0:T(8,128)(2,1)} %bitcast.2) | data formatting | bytes 262144

commit v3 on v2

--- a/solution.py
+++ b/solution.py
@@ -17,7 +17,7 @@
 
 BATCHES = 4
 SLOTS = TREE // BATCHES
-PLACES = (0, 3, 6, 7, 14, 21, 23, 26, 30)
+PLACES = (0, 3, 6, 7, 13, 19, 21, 24, 28)
 OFFSET = 2
 KEY_BLOCK = 1024
 NX, NY, NZ = 4, 2, 8
@@ -41,7 +41,7 @@
     draft, gain, w_query, w_keyval, w_out, cache, parents_in, counts, lengths, out,
     parents, rows, gains, w_in, w_o, keys, values, values_t, part, sums, sq_send, sq_recv,
     keys_new, values_new, reach, scores, heads, outp, out1, merged, out2, handed,
-    send, recv, local, sib_send, sib_recv,
+    send, recv, local, sib_send, sib_recv, out_sem,
 ):
     T = SLOTS
     sec = lax.axis_index("section")
@@ -63,7 +63,7 @@
         return to_chip, to_core, (sec, to_chip * 2 + to_core, z)
 
     other_section = (1 - sec, req, z)
-    offsets = [(dx, dy) for dx in range(NX) for dy in range(NY)]
+    offsets = [(2, 1), (2, 0), (1, 1), (3, 1), (1, 0), (3, 0), (0, 1), (0, 0)]
     near = (1, -1, 2, -2)
 
     def push(src, dst, phase, m, device):
@@ -260,10 +260,10 @@
         product = product.reshape(2, CHIPS, T, product.shape[1])
         for i in range(2):
             outp[m, :, i] = product[i]
+        push(outp.at[m, (z + 4) % NZ, 0], out1.at[m, 2, 0], OUT1, m, along(2))
+        push(outp.at[m, (z + 4) % NZ, 1], out1.at[m, 2, 1], OUT1, m, along(-2))
         push(outp.at[m, (z + 3) % NZ], out1.at[m, 0], OUT1, m, along(1))
         push(outp.at[m, (z + 5) % NZ], out1.at[m, 1], OUT1, m, along(-1))
-        push(outp.at[m, (z + 4) % NZ, 0], out1.at[m, 2, 0], OUT1, m, along(2))
-        push(outp.at[m, (z + 4) % NZ, 1], out1.at[m, 2, 1], OUT1, m, along(-2))
         push(outp.at[m, (z + 1) % NZ], out2.at[m, 2], OUT2, m, along(1))
         push(outp.at[m, (z + 7) % NZ], out2.at[m, 3], OUT2, m, along(-1))
 
@@ -281,12 +281,16 @@
         for k in range(4):
             total = total + out2[m, k].astype(F32)
         result = (total + rows[m, core, OWN].astype(F32)).astype(BF16)
-        out[:, pl.ds(pl.multiple_of(m * T, T), T), :] = result
+        handed[m] = result
 
         @pl.when(sec == 0)
         def _():
-            handed[m] = result
             push(handed.at[m], rows.at[m, core, OWN], HAND, m, other_section)
+        write(m).start()
+
+    def write(m):
+        return pltpu.make_async_copy(
+            handed.at[m], out.at[:, pl.ds(pl.multiple_of(m * T, T), T)], out_sem.at[m])
 
     steps = [step_rows, step_pass, step_last_rows, step_project, step_attend,
              step_heads, step_out, step_merge, step_finish]
@@ -305,6 +309,7 @@
     lax.fori_loop(0, PLACES[-1] + (BATCHES - 1) * OFFSET + 1, tick, 0)
 
     def drain(m, carry):
+        write(m).wait()
         await_bytes(rows.at[0, 0, pl.ds(0, 4)], send.at[m, ROWS1])
         await_bytes(rows.at[0, 0, pl.ds(0, 3)], send.at[m, ROWS2])
         await_bytes(rows.at[0, 0], send.at[m, ROWS_SIB])
@@ -337,7 +342,7 @@
         kernel,
         out_shape=jax.ShapeDtypeStruct((2, TREE, feats), BF16),
         in_specs=[anywhere, vmem, anywhere, anywhere, anywhere, anywhere, anywhere, smem, smem],
-        out_specs=vmem,
+        out_specs=anywhere,
         scratch_shapes=[
             pltpu.VMEM((1, TREE), jnp.int32),
             pltpu.VMEM((N, 2, NZ, 2, T, feats), BF16),
@@ -366,6 +371,7 @@
             pltpu.SemaphoreType.DMA((6,)),
             pltpu.SemaphoreType.DMA((3,)),
             pltpu.SemaphoreType.DMA((3,)),
+            pltpu.SemaphoreType.DMA((N,)),
         ],
         compiler_params=pltpu.CompilerParams(
             collective_id=0, has_side_effects=True, vmem_limit_bytes=58 << 20),

time: 118 us -> 115 us (0.975)
  Pallas kernels: 115 us -> 112 us
    pallas_call x1, Pallas kernels: 115 us -> 112 us  [body(): pl.pallas_call(kernel, out_shape=jax.ShapeDtypeStruct((2, TREE, feats), B...]
where the time goes in v3:
time: 115 us
  Pallas kernels  112 us (97%)
  local copies, waits for them, and re-layouts  1.57 us (1%)
  between operations  1.3 us (1%)
    pallas_call x1, Pallas kernels, body(): pl.pallas_call(kernel, out_shape=jax.ShapeDtypeStruct((2, TREE, feats), B...  112 us

profile of v3, /device:TPU:8, one launch (start us, length us, event | category | flops | bytes accessed | tf_op | source)
XLA Modules:
  0.0 114.8 jit_solution(10389151295026920032)
XLA Ops:
  1.3 111.9 %two_layers.1 = bf16[2,64,512]{2,1,0:T(8,128)(2,1)} custom-call(bf16[2,64,512]{2,1,0:T(8,128)(2,1)} %bitcast.3, bf16[1,512]{1,0:T(2,128)(2,1)} %gain.1, bf16[1,512,1024]{2,1,0:T(8,128)(2,1)} %w_query.1, bf16[1,2,512,128]{3,2,1,0:T(8,128)(2,1)} %w_keyval.1, bf16[1,1024,512]{2,1,0:T(8,128)(2,1)} %w_out.1, bf16[1,1,2,4096,128]{4,3,2,1,0:T(8,128)(2,1)} %cache.1, ...), custom_call_target="tpu_custom_call" | custom-call | tf_op jit(solution)/shard_map/two_layers/pallas_call | solution.py:341
  113.2 1.6 %copy.13 = bf16[1,128,512]{2,1,0:T(8,128)(2,1)} copy(bf16[1,128,512]{2,1,0:T(8,128)(2,1)} %bitcast.2) | data formatting | bytes 262144

commit v4 on v3

--- a/solution.py
+++ b/solution.py
@@ -17,7 +17,7 @@
 
 BATCHES = 4
 SLOTS = TREE // BATCHES
-PLACES = (0, 3, 6, 7, 13, 19, 21, 24, 28)
+PLACES = (0, 3, 6, 7, 13, 19, 20, 23, 27)
 OFFSET = 2
 KEY_BLOCK = 1024
 NX, NY, NZ = 4, 2, 8
@@ -39,7 +39,7 @@
 
 def kernel(
     draft, gain, w_query, w_keyval, w_out, cache, parents_in, counts, lengths, out,
-    parents, rows, gains, w_in, w_o, keys, values, values_t, part, sums, sq_send, sq_recv,
+    parents, rows, gains, w_in, w_o, keys, values, values_t, half_sum, half_sq, part, sums, sq_send, sq_recv,
     keys_new, values_new, reach, scores, heads, outp, out1, merged, out2, handed,
     send, recv, local, sib_send, sib_recv, out_sem,
 ):
@@ -166,22 +166,22 @@
         push(rows.at[m, core, 4, 1], rows.at[m, core, 6, 1], ROWS2, m, along(-2))
         push(rows.at[m, core, pl.ds(0, 5)], rows.at[m, core, pl.ds(0, 5)], ROWS_SIB, m, sibling)
 
+    def project_half(m, i):
+        block = rows[m, i].reshape(CHIPS * 2 * T, rows.shape[-1]).astype(F32)
+        scaled = (block * gains[i, 0:1, :]).astype(BF16)
+        return dot(scaled, w_in[i]), jnp.sum(block * block, axis=1, keepdims=True)
+
     def step_last_rows(m):
         await_bytes(rows.at[0, 0, pl.ds(0, 3)], recv.at[m, ROWS2])
         push(rows.at[m, core, pl.ds(5, 3)], rows.at[m, core, pl.ds(5, 3)], ROWS_SIB, m, sibling)
+        pl.when(m == 0)(weights_ready)
+        half_sum[m], half_sq[m] = project_half(m, core)
 
     def step_project(m):
         await_bytes(rows.at[0, 0], recv.at[m, ROWS_SIB])
-        pl.when(m == 0)(weights_ready)
-        total_sq = None
-        total = None
-        for s in range(2):
-            block = rows[m, s].reshape(CHIPS * 2 * T, rows.shape[-1]).astype(F32)
-            sq = jnp.sum(block * block, axis=1, keepdims=True)
-            scaled = (block * gains[s, 0:1, :]).astype(BF16)
-            product = dot(scaled, w_in[s])
-            total = product if total is None else total + product
-            total_sq = sq if total_sq is None else total_sq + sq
+        total, total_sq = project_half(m, 1 - core)
+        total = total + half_sum[m]
+        total_sq = total_sq + half_sq[m]
         part[m] = total.reshape(CHIPS, 2, T, total.shape[1]).astype(BF16)
         wide = jnp.broadcast_to(total_sq, (CHIPS * 2 * T, HEAD_DIM))
         lane = lax.broadcasted_iota(jnp.int32, wide.shape, 1)
@@ -250,16 +250,18 @@
             if (dx, dy) != (0, 0):
                 push(heads.at[m, core, chip], heads.at[m, core, chip], HEADS, m, planar(dx, dy, 0)[2])
 
+    def out_half(m, i):
+        product = dot(heads[m, i].reshape(CHIPS * T, heads.shape[-1]), w_o[...]).astype(BF16)
+        outp[m, :, i] = product.reshape(CHIPS, T, product.shape[1])
+
     def step_heads(m):
         await_bytes(heads.at[0, 0, pl.ds(0, 7)], recv.at[m, HEADS])
         push(heads.at[m, core], heads.at[m, core], HEADS_SIB, m, sibling)
+        out_half(m, core)
 
     def step_out(m):
         await_bytes(heads.at[0, 0], recv.at[m, HEADS_SIB])
-        product = dot(heads[m].reshape(2 * CHIPS * T, heads.shape[-1]), w_o[...]).astype(BF16)
-        product = product.reshape(2, CHIPS, T, product.shape[1])
-        for i in range(2):
-            outp[m, :, i] = product[i]
+        out_half(m, 1 - core)
         push(outp.at[m, (z + 4) % NZ, 0], out1.at[m, 2, 0], OUT1, m, along(2))
         push(outp.at[m, (z + 4) % NZ, 1], out1.at[m, 2, 1], OUT1, m, along(-2))
         push(outp.at[m, (z + 3) % NZ], out1.at[m, 0], OUT1, m, along(1))
@@ -352,6 +354,8 @@
             pltpu.VMEM((positions, HEAD_DIM), BF16),
             pltpu.VMEM((positions, HEAD_DIM), BF16),
             pltpu.VMEM((blocks, HEAD_DIM, KEY_BLOCK), BF16),
+            pltpu.VMEM((N, CHIPS * 2 * T, half), F32),
+            pltpu.VMEM((N, CHIPS * 2 * T, 1), F32),
             pltpu.VMEM((N, CHIPS, 2, T, half), BF16),
             pltpu.VMEM((N, 2 * CHIPS, T, half), BF16),
             pltpu.VMEM((N, CHIPS, 2, T, HEAD_DIM), BF16),

time: 115 us -> 115 us (level)
  no operation moved by 1% of the time
where the time goes in v4:
time: 115 us
  Pallas kernels  112 us (97%)
  local copies, waits for them, and re-layouts  1.57 us (1%)
  between operations  1.3 us (1%)
    pallas_call x1, Pallas kernels, body(): pl.pallas_call(kernel, out_shape=jax.ShapeDtypeStruct((2, TREE, feats), B...  112 us

profile of v4, /device:TPU:8, one launch (start us, length us, event | category | flops | bytes accessed | tf_op | source)
XLA Modules:
  0.0 115.4 jit_solution(12169992395937611489)
XLA Ops:
  1.3 112.5 %two_layers.1 = bf16[2,64,512]{2,1,0:T(8,128)(2,1)} custom-call(bf16[2,64,512]{2,1,0:T(8,128)(2,1)} %bitcast.3, bf16[1,512]{1,0:T(2,128)(2,1)} %gain.1, bf16[1,512,1024]{2,1,0:T(8,128)(2,1)} %w_query.1, bf16[1,2,512,128]{3,2,1,0:T(8,128)(2,1)} %w_keyval.1, bf16[1,1024,512]{2,1,0:T(8,128)(2,1)} %w_out.1, bf16[1,1,2,4096,128]{4,3,2,1,0:T(8,128)(2,1)} %cache.1, ...), custom_call_target="tpu_custom_call" | custom-call | tf_op jit(solution)/shard_map/two_layers/pallas_call | solution.py:343
  113.8 1.6 %copy.13 = bf16[1,128,512]{2,1,0:T(8,128)(2,1)} copy(bf16[1,128,512]{2,1,0:T(8,128)(2,1)} %bitcast.2) | data formatting | bytes 262144
